TPU v7x, 32 devices: a whole 2x2x4 slice. The times are simulated.
32 devices in a mesh: dp: 8 (over y, x, core), tensor: 4 (over z).
Axes of the slice: x: 2, y: 2, z: 4, core: 2. Of those that a mesh axis runs over, the one named last changes fastest.
Arguments:
- hidden: bfloat16 [4096, 8192], P(('dp', 'tensor')), may hold values from -6 to 6
- norm_gain: float32 [8192], replicated, may hold values from 0.5 to 1.5
- tile_values: bfloat16 [4, 80, 128, 128], P('tensor', 'dp'), may hold values from -0.15625 to 0.15625
- tile_ids: int32 [4, 80], P('tensor', 'dp'), may hold values from 0 to 1279, as said below
- tile_counts: int32 [4, 8], P('tensor', 'dp'), may hold values from 5 to 10, as said below
- proj_grad: bfloat16 [4096, 10240], P('dp', 'tensor'), may hold values from -6 to 6
Outputs:
- projections: bfloat16 [4096, 10240], P('dp', 'tensor')
- hidden_grad: bfloat16 [4096, 8192], P(('dp', 'tensor'))
- tile_grads: float32 [4, 80, 128, 128], P('tensor', 'dp')
- gain_grad: float32 [8192], replicated
Inputs may be any that keep to these rules, and one draw needn't show every extreme that they name: `tile_ids`: within each tensor index the 80 block numbers are distinct; a slot's number holds whether or not the slot is live. `tile_counts`: for every tensor index some owner has all 10 slots live.
All inputs are finite; a program needn't handle non-finite values.
Results may differ from a plain program's by a relative error of at most 0.013.
Values may be sent and summed in bfloat16 or wider, within the bound.
A program may use at most 192 MiB of HBM per device.

v0:
```python
import math
import jax
import jax.numpy as jnp
from jax import lax
from jax.sharding import PartitionSpec as P

EPSILON = 1e-05


def normalize(source, norm_gain):
    source_f = source.astype(jnp.float32)
    inverse = lax.rsqrt(jnp.mean(source_f * source_f, axis=-1, keepdims=True) + EPSILON)
    return (source_f, inverse, (source_f * inverse * norm_gain).astype(jnp.bfloat16))


def selector(block_names, total_count):
    return (block_names[:, None] == jnp.arange(total_count, dtype=jnp.int32)[None, :]).astype(
        jnp.bfloat16
    )


def pick_tiles(blocks, block_names, total_count):
    chooser = selector(block_names, total_count)
    return jnp.einsum("nri,sr->nsi", blocks, chooser, preferred_element_type=jnp.float32).astype(
        jnp.bfloat16
    )


def place_tiles(values, block_names, total_count):
    chooser = selector(block_names, total_count)
    upper_half = values.astype(jnp.bfloat16)
    lower_half = (values - upper_half.astype(jnp.float32)).astype(jnp.bfloat16)
    placed = jnp.einsum("nsi,sr->nri", upper_half, chooser, preferred_element_type=jnp.float32)
    return placed + jnp.einsum(
        "nsi,sr->nri", lower_half, chooser, preferred_element_type=jnp.float32
    )


def over_groups(handler, running, tile_block, tile_names, anchor, slot_count):
    group_total = tile_names.shape[0] // slot_count

    def loop_step(group_idx, state):
        offset = group_idx * slot_count
        block_vals = lax.dynamic_slice_in_dim(tile_block, offset, slot_count, 0)
        block_names = lax.dynamic_slice_in_dim(tile_names, offset, slot_count, 0)
        return handler(state, block_vals, block_names, anchor + offset)

    return lax.fori_loop(0, group_total, loop_step, running)


def body(hidden, norm_gain, tile_values, tile_ids, tile_counts, proj_grad):
    model_width = hidden.shape[1]
    tile_size = tile_values.shape[-1]
    slot_count = tile_values.shape[1]
    seq_rows = proj_grad.shape[0]
    col_tiles = proj_grad.shape[1] // tile_size
    row_tiles = model_width // tile_size
    live_mask = (jnp.arange(slot_count) < tile_counts[0, 0]).astype(jnp.bfloat16)
    masked = tile_values[0] * live_mask[:, None, None]
    own_names = tile_ids[0]
    hidden_f, inverse, normed = normalize(hidden, norm_gain)
    gathered = lax.all_gather(normed, "tensor", axis=0, tiled=True)
    x_blocks = gathered.reshape(seq_rows, row_tiles, tile_size)
    g_blocks = proj_grad.reshape(seq_rows, col_tiles, tile_size)

    def forward_group(running, block_vals, block_names, offset):
        picked = pick_tiles(x_blocks, block_names // col_tiles, row_tiles)
        parts = jnp.einsum("nsi,sij->nsj", picked, block_vals, preferred_element_type=jnp.float32)
        return running + place_tiles(parts, block_names % col_tiles, col_tiles)

    start_out = jnp.zeros((seq_rows, col_tiles, tile_size), jnp.float32)
    all_vals, all_names = (
        lax.all_gather(masked, "dp", axis=0, tiled=True),
        lax.all_gather(own_names, "dp", axis=0, tiled=True),
    )
    outputs = over_groups(forward_group, start_out, all_vals, all_names, 0, slot_count)
    projections = outputs.reshape(seq_rows, col_tiles * tile_size).astype(jnp.bfloat16)
    slot_total_all = all_names.shape[0]

    def row_grad_of(g_part):

        def backward_group(local_grad, block_vals, block_names, offset):
            picked_g = pick_tiles(g_part, block_names % col_tiles, col_tiles)
            backward = jnp.einsum(
                "nsj,sij->nsi", picked_g, block_vals, preferred_element_type=jnp.float32
            )
            return local_grad + place_tiles(backward, block_names // col_tiles, row_tiles)

        start_grad = jnp.zeros((g_part.shape[0], row_tiles, tile_size), jnp.float32)
        local_grad = over_groups(backward_group, start_grad, all_vals, all_names, 0, slot_count)
        return local_grad.reshape(g_part.shape[0], model_width).astype(jnp.bfloat16)

    def tile_grad_of(weight_grad, x_part, g_part):

        def tile_group(tile_acc, block_vals, block_names, offset):
            picked_x = pick_tiles(x_part, block_names // col_tiles, row_tiles)
            picked_g = pick_tiles(g_part, block_names % col_tiles, col_tiles)
            tile_part = jnp.einsum(
                "nsi,nsj->sij", picked_x, picked_g, preferred_element_type=jnp.float32
            )
            current = lax.dynamic_slice_in_dim(tile_acc, offset, tile_part.shape[0], 0)
            return lax.dynamic_update_slice_in_dim(tile_acc, current + tile_part, offset, 0)

        return over_groups(tile_group, weight_grad, all_vals, all_names, 0, slot_count)

    block_rows = math.gcd(seq_rows, 256)
    start_tiles = jnp.zeros((slot_total_all, tile_size, tile_size), jnp.float32)

    def row_block(block_idx, state):
        row_grad, weight_grad = state
        begin = block_idx * block_rows
        x_part = lax.dynamic_slice_in_dim(x_blocks, begin, block_rows, 0)
        g_part = lax.dynamic_slice_in_dim(g_blocks, begin, block_rows, 0)
        rounded = row_grad_of(g_part)
        row_grad = lax.dynamic_update_slice_in_dim(row_grad, rounded, begin, 0)
        weight_grad = tile_grad_of(weight_grad, x_part, g_part)
        return (row_grad, weight_grad)

    initial_back = (jnp.zeros((seq_rows, model_width), jnp.bfloat16), start_tiles)
    row_grad, weight_grad = lax.fori_loop(0, seq_rows // block_rows, row_block, initial_back)
    row_sum = lax.psum_scatter(row_grad, "tensor", scatter_dimension=0, tiled=True).astype(
        jnp.float32
    )
    tile_sum = lax.psum_scatter(
        weight_grad.astype(jnp.bfloat16), "dp", scatter_dimension=0, tiled=True
    ).astype(jnp.float32)
    tile_grads = (tile_sum * live_mask.astype(jnp.float32)[:, None, None])[None]
    unit = hidden_f * inverse
    gain_part = jnp.sum(row_sum * unit, axis=0)
    gain_grad = lax.psum(gain_part, ("dp", "tensor"))
    scaled = row_sum * norm_gain
    hidden_grad = (
        inverse * (scaled - unit * jnp.mean(scaled * unit, axis=-1, keepdims=True))
    ).astype(jnp.bfloat16)
    return (projections, hidden_grad, tile_grads, gain_grad)


def solution(mesh):
    in_specs = (
        P(("dp", "tensor"), None),
        P(),
        P("tensor", "dp", None, None),
        P("tensor", "dp"),
        P("tensor", "dp"),
        P("dp", "tensor"),
    )
    out_specs = (P("dp", "tensor"), P(("dp", "tensor"), None), P("tensor", "dp", None, None), P())
    return jax.shard_map(body, mesh=mesh, in_specs=in_specs, out_specs=out_specs, check_vma=False)
```

profile of v0, /device:TPU:0, one launch (start us, length us, event | category | flops | bytes accessed | tf_op | source)
XLA Modules:
  0.0 951.3 jit_solution(16404277503629230293)
XLA Ops:
  20.3 9.5 all-reduce
  29.8 135.6 %all-gather.6.cloned.1.call-done = bf16[512,8192]{1,0:T(8,128)(2,1)} async-done(((bf16[128,8192]{1,0:T(8,128)(2,1)}), bf16[512,8192]{1,0:T(8,128)(2,1)}) %all-gather.6.cloned.1.call-update) | async-done | bytes 8388624 | tf_op jit(solution)/shard_map/all_gather | solution.py:62
  165.4 9.4 copy.42
  174.7 21.4 %all-gather.4.cloned.1.call-done = bf16[80,128,128]{2,1,0:T(8,128)(2,1)} async-done(((bf16[10,128,128]{2,1,0:T(8,128)(2,1)}), bf16[80,128,128]{2,1,0:T(8,128)(2,1)}) %all-gather.4.cloned.1.call-update) | async-done | bytes 2621456 | tf_op jit(solution)/shard_map/all_gather | solution.py:73
  203.4 463.0 %while.101 = (s32[]{:T(128)}, bf16[512,8192]{1,0:T(8,128)(2,1)}, f32[80,128,128]{2,1,0:T(8,128)}, bf16[512,20,128]{0,2,1:T(8,128)(2,1)}, s32[80]{0:T(128)S(1)}, ...) while((s32[]{:T(128)}, bf16[512,8192]{1,0:T(8,128)(2,1)}, ...), condition=%wide.region_8.9_spmd, body=%wide.region_3.8_spmd.sunk | while | flops 330664448 | bytes 85787744 | solution.py:120
  205.9 162.2 %while.103 = (s32[]{:T(128)}, f32[256,64,128]{2,1,0:T(8,128)}, s32[80]{0:T(128)S(1)}, bf16[80,128,128]{2,1,0:T(8,128)(2,1)}, bf16[256,20,128]{2,1,0:T(8,128)(2,1...) while((s32[]{:T(128)}, f32[256,64,128]{2,1,0:T(8,128)}, s32[80]{0:T(128)S(1)}, ...), condition=%wide.region_5.5_spmd.clone, body=%wide.region_4.4_spmd.clone.sunk | while | flops 188810816 | bytes 41746828 | solution.py:48
  216.1 8.0 bitcast_add_fusion.5
  234.3 10.4 %bitcast_add_fusion.5 = f32[256,64,128]{2,1,0:T(8,128)} fusion(f32[256,64,128]{2,1,0:T(8,128)} %get-tuple-element.990, f32[64,256,128]{2,0,1:T(8,128)} %fusion.97, pred[]{:T(512)S(6)} %compare.7, bf16[256,10,128]{2,1,0:T(8,128)(2,1)S(1)} %copy.73, s32[10]{0:T(128)S(1)} %get-tuple-element.971), kind=kOutput, calls=%fused_computation.16.clone.1 | convolution fusion | flops 48235136 | bytes 25821224 | tf_op jit(solution)/shard_map/while/body/eval_jaxpr/while/body/eval_jaxpr/nsi,sr->nri/dot_general | solution.py:34
  254.8 10.4 %bitcast_add_fusion.5 = f32[256,64,128]{2,1,0:T(8,128)} fusion(f32[256,64,128]{2,1,0:T(8,128)} %get-tuple-element.990, f32[64,256,128]{2,0,1:T(8,128)} %fusion.97, pred[]{:T(512)S(6)} %compare.7, bf16[256,10,128]{2,1,0:T(8,128)(2,1)S(1)} %copy.73, s32[10]{0:T(128)S(1)} %get-tuple-element.971), kind=kOutput, calls=%fused_computation.16.clone.1 | convolution fusion | flops 48235136 | bytes 25821224 | tf_op jit(solution)/shard_map/while/body/eval_jaxpr/while/body/eval_jaxpr/nsi,sr->nri/dot_general | solution.py:34
  275.4 10.4 %bitcast_add_fusion.5 = f32[256,64,128]{2,1,0:T(8,128)} fusion(f32[256,64,128]{2,1,0:T(8,128)} %get-tuple-element.990, f32[64,256,128]{2,0,1:T(8,128)} %fusion.97, pred[]{:T(512)S(6)} %compare.7, bf16[256,10,128]{2,1,0:T(8,128)(2,1)S(1)} %copy.73, s32[10]{0:T(128)S(1)} %get-tuple-element.971), kind=kOutput, calls=%fused_computation.16.clone.1 | convolution fusion | flops 48235136 | bytes 25821224 | tf_op jit(solution)/shard_map/while/body/eval_jaxpr/while/body/eval_jaxpr/nsi,sr->nri/dot_general | solution.py:34
  296.0 10.4 %bitcast_add_fusion.5 = f32[256,64,128]{2,1,0:T(8,128)} fusion(f32[256,64,128]{2,1,0:T(8,128)} %get-tuple-element.990, f32[64,256,128]{2,0,1:T(8,128)} %fusion.97, pred[]{:T(512)S(6)} %compare.7, bf16[256,10,128]{2,1,0:T(8,128)(2,1)S(1)} %copy.73, s32[10]{0:T(128)S(1)} %get-tuple-element.971), kind=kOutput, calls=%fused_computation.16.clone.1 | convolution fusion | flops 48235136 | bytes 25821224 | tf_op jit(solution)/shard_map/while/body/eval_jaxpr/while/body/eval_jaxpr/nsi,sr->nri/dot_general | solution.py:34
  316.5 10.4 %bitcast_add_fusion.5 = f32[256,64,128]{2,1,0:T(8,128)} fusion(f32[256,64,128]{2,1,0:T(8,128)} %get-tuple-element.990, f32[64,256,128]{2,0,1:T(8,128)} %fusion.97, pred[]{:T(512)S(6)} %compare.7, bf16[256,10,128]{2,1,0:T(8,128)(2,1)S(1)} %copy.73, s32[10]{0:T(128)S(1)} %get-tuple-element.971), kind=kOutput, calls=%fused_computation.16.clone.1 | convolution fusion | flops 48235136 | bytes 25821224 | tf_op jit(solution)/shard_map/while/body/eval_jaxpr/while/body/eval_jaxpr/nsi,sr->nri/dot_general | solution.py:34
  337.1 10.4 %bitcast_add_fusion.5 = f32[256,64,128]{2,1,0:T(8,128)} fusion(f32[256,64,128]{2,1,0:T(8,128)} %get-tuple-element.990, f32[64,256,128]{2,0,1:T(8,128)} %fusion.97, pred[]{:T(512)S(6)} %compare.7, bf16[256,10,128]{2,1,0:T(8,128)(2,1)S(1)} %copy.73, s32[10]{0:T(128)S(1)} %get-tuple-element.971), kind=kOutput, calls=%fused_computation.16.clone.1 | convolution fusion | flops 48235136 | bytes 25821224 | tf_op jit(solution)/shard_map/while/body/eval_jaxpr/while/body/eval_jaxpr/nsi,sr->nri/dot_general | solution.py:34
  357.7 10.4 %bitcast_add_fusion.5 = f32[256,64,128]{2,1,0:T(8,128)} fusion(f32[256,64,128]{2,1,0:T(8,128)} %get-tuple-element.990, f32[64,256,128]{2,0,1:T(8,128)} %fusion.97, pred[]{:T(512)S(6)} %compare.7, bf16[256,10,128]{2,1,0:T(8,128)(2,1)S(1)} %copy.73, s32[10]{0:T(128)S(1)} %get-tuple-element.971), kind=kOutput, calls=%fused_computation.16.clone.1 | convolution fusion | flops 48235136 | bytes 25821224 | tf_op jit(solution)/shard_map/while/body/eval_jaxpr/while/body/eval_jaxpr/nsi,sr->nri/dot_general | solution.py:34
  372.5 10.0 %bitcast_dynamic-update-slice_fusion.3 = bf16[512,8192]{1,0:T(8,128)(2,1)} fusion(bf16[512,8192]{1,0:T(8,128)(2,1)} %get-tuple-element.1081, s32[]{:T(128)S(6)} %select_n.148, bf16[32,8,64,128]{3,2,1,0:T(8,128)(2,1)S(1)} %bitcast.116), kind=kLoop, calls=%fused_computation.34.clone.1 | loop fusion | bytes 8388612 | tf_op jit(solution)/shard_map/while/body/eval_jaxpr/dynamic_update_slice | solution.py:115
  382.6 5.2 constant_dynamic-slice_fusion.5
  387.7 47.1 %while.104 = (s32[]{:T(128)}, f32[80,128,128]{2,1,0:T(8,128)}, s32[80]{0:T(128)S(1)}, bf16[256,64,128]{2,1,0:T(8,128)(2,1)}, bf16[256,20,128]{2,1,0:T(8,128)(2,1...) while((s32[]{:T(128)}, f32[80,128,128]{2,1,0:T(8,128)}, s32[80]{0:T(128)S(1)}, ...), condition=%wide.region_7.7_spmd, body=%wide.region_6.6_spmd.sunk | while | flops 139756480 | bytes 9437531 | solution.py:48
  437.4 162.2 %while.103 = (s32[]{:T(128)}, f32[256,64,128]{2,1,0:T(8,128)}, s32[80]{0:T(128)S(1)}, bf16[80,128,128]{2,1,0:T(8,128)(2,1)}, bf16[256,20,128]{2,1,0:T(8,128)(2,1...) while((s32[]{:T(128)}, f32[256,64,128]{2,1,0:T(8,128)}, s32[80]{0:T(128)S(1)}, ...), condition=%wide.region_5.5_spmd.clone, body=%wide.region_4.4_spmd.clone.sunk | while | flops 188810816 | bytes 41746828 | solution.py:48
  447.6 8.0 bitcast_add_fusion.5
  465.7 10.4 %bitcast_add_fusion.5 = f32[256,64,128]{2,1,0:T(8,128)} fusion(f32[256,64,128]{2,1,0:T(8,128)} %get-tuple-element.990, f32[64,256,128]{2,0,1:T(8,128)} %fusion.97, pred[]{:T(512)S(6)} %compare.7, bf16[256,10,128]{2,1,0:T(8,128)(2,1)S(1)} %copy.73, s32[10]{0:T(128)S(1)} %get-tuple-element.971), kind=kOutput, calls=%fused_computation.16.clone.1 | convolution fusion | flops 48235136 | bytes 25821224 | tf_op jit(solution)/shard_map/while/body/eval_jaxpr/while/body/eval_jaxpr/nsi,sr->nri/dot_general | solution.py:34
  486.3 10.4 %bitcast_add_fusion.5 = f32[256,64,128]{2,1,0:T(8,128)} fusion(f32[256,64,128]{2,1,0:T(8,128)} %get-tuple-element.990, f32[64,256,128]{2,0,1:T(8,128)} %fusion.97, pred[]{:T(512)S(6)} %compare.7, bf16[256,10,128]{2,1,0:T(8,128)(2,1)S(1)} %copy.73, s32[10]{0:T(128)S(1)} %get-tuple-element.971), kind=kOutput, calls=%fused_computation.16.clone.1 | convolution fusion | flops 48235136 | bytes 25821224 | tf_op jit(solution)/shard_map/while/body/eval_jaxpr/while/body/eval_jaxpr/nsi,sr->nri/dot_general | solution.py:34
  506.9 10.4 %bitcast_add_fusion.5 = f32[256,64,128]{2,1,0:T(8,128)} fusion(f32[256,64,128]{2,1,0:T(8,128)} %get-tuple-element.990, f32[64,256,128]{2,0,1:T(8,128)} %fusion.97, pred[]{:T(512)S(6)} %compare.7, bf16[256,10,128]{2,1,0:T(8,128)(2,1)S(1)} %copy.73, s32[10]{0:T(128)S(1)} %get-tuple-element.971), kind=kOutput, calls=%fused_computation.16.clone.1 | convolution fusion | flops 48235136 | bytes 25821224 | tf_op jit(solution)/shard_map/while/body/eval_jaxpr/while/body/eval_jaxpr/nsi,sr->nri/dot_general | solution.py:34
  527.4 10.4 %bitcast_add_fusion.5 = f32[256,64,128]{2,1,0:T(8,128)} fusion(f32[256,64,128]{2,1,0:T(8,128)} %get-tuple-element.990, f32[64,256,128]{2,0,1:T(8,128)} %fusion.97, pred[]{:T(512)S(6)} %compare.7, bf16[256,10,128]{2,1,0:T(8,128)(2,1)S(1)} %copy.73, s32[10]{0:T(128)S(1)} %get-tuple-element.971), kind=kOutput, calls=%fused_computation.16.clone.1 | convolution fusion | flops 48235136 | bytes 25821224 | tf_op jit(solution)/shard_map/while/body/eval_jaxpr/while/body/eval_jaxpr/nsi,sr->nri/dot_general | solution.py:34
  548.0 10.4 %bitcast_add_fusion.5 = f32[256,64,128]{2,1,0:T(8,128)} fusion(f32[256,64,128]{2,1,0:T(8,128)} %get-tuple-element.990, f32[64,256,128]{2,0,1:T(8,128)} %fusion.97, pred[]{:T(512)S(6)} %compare.7, bf16[256,10,128]{2,1,0:T(8,128)(2,1)S(1)} %copy.73, s32[10]{0:T(128)S(1)} %get-tuple-element.971), kind=kOutput, calls=%fused_computation.16.clone.1 | convolution fusion | flops 48235136 | bytes 25821224 | tf_op jit(solution)/shard_map/while/body/eval_jaxpr/while/body/eval_jaxpr/nsi,sr->nri/dot_general | solution.py:34
  568.6 10.4 %bitcast_add_fusion.5 = f32[256,64,128]{2,1,0:T(8,128)} fusion(f32[256,64,128]{2,1,0:T(8,128)} %get-tuple-element.990, f32[64,256,128]{2,0,1:T(8,128)} %fusion.97, pred[]{:T(512)S(6)} %compare.7, bf16[256,10,128]{2,1,0:T(8,128)(2,1)S(1)} %copy.73, s32[10]{0:T(128)S(1)} %get-tuple-element.971), kind=kOutput, calls=%fused_computation.16.clone.1 | convolution fusion | flops 48235136 | bytes 25821224 | tf_op jit(solution)/shard_map/while/body/eval_jaxpr/while/body/eval_jaxpr/nsi,sr->nri/dot_general | solution.py:34
  589.1 10.4 %bitcast_add_fusion.5 = f32[256,64,128]{2,1,0:T(8,128)} fusion(f32[256,64,128]{2,1,0:T(8,128)} %get-tuple-element.990, f32[64,256,128]{2,0,1:T(8,128)} %fusion.97, pred[]{:T(512)S(6)} %compare.7, bf16[256,10,128]{2,1,0:T(8,128)(2,1)S(1)} %copy.73, s32[10]{0:T(128)S(1)} %get-tuple-element.971), kind=kOutput, calls=%fused_computation.16.clone.1 | convolution fusion | flops 48235136 | bytes 25821224 | tf_op jit(solution)/shard_map/while/body/eval_jaxpr/while/body/eval_jaxpr/nsi,sr->nri/dot_general | solution.py:34
  604.0 10.1 %bitcast_dynamic-update-slice_fusion.3 = bf16[512,8192]{1,0:T(8,128)(2,1)} fusion(bf16[512,8192]{1,0:T(8,128)(2,1)} %get-tuple-element.1081, s32[]{:T(128)S(6)} %select_n.148, bf16[32,8,64,128]{3,2,1,0:T(8,128)(2,1)S(1)} %bitcast.116), kind=kLoop, calls=%fused_computation.34.clone.1 | loop fusion | bytes 8388612 | tf_op jit(solution)/shard_map/while/body/eval_jaxpr/dynamic_update_slice | solution.py:115
  614.1 5.2 constant_dynamic-slice_fusion.5
  619.2 47.1 %while.104 = (s32[]{:T(128)}, f32[80,128,128]{2,1,0:T(8,128)}, s32[80]{0:T(128)S(1)}, bf16[256,64,128]{2,1,0:T(8,128)(2,1)}, bf16[256,20,128]{2,1,0:T(8,128)(2,1...) while((s32[]{:T(128)}, f32[80,128,128]{2,1,0:T(8,128)}, s32[80]{0:T(128)S(1)}, ...), condition=%wide.region_7.7_spmd, body=%wide.region_6.6_spmd.sunk | while | flops 139756480 | bytes 9437531 | solution.py:48
  671.5 213.0 %while.102 = (s32[]{:T(128)}, f32[512,20,128]{2,1,0:T(8,128)}, s32[80]{0:T(128)S(1)}, bf16[80,128,128]{2,1,0:T(8,128)(2,1)}, bf16[512,64,128]{2,1,0:T(8,128)(2,1...) while((s32[]{:T(128)}, f32[512,20,128]{2,1,0:T(8,128)}, s32[80]{0:T(128)S(1)}, ...), condition=%wide.region_2.3_spmd.clone, body=%wide.region_1.2_spmd.clone.sunk | while | flops 311297152 | bytes 42795404 | solution.py:48
  681.1 5.4 fusion.89
  689.4 7.4 bitcast_add_fusion.4
  706.5 5.3 fusion.89
  714.7 9.2 bitcast_add_fusion.4
  733.5 5.3 fusion.89
  741.7 9.0 bitcast_add_fusion.4
  760.3 5.3 fusion.89
  768.5 9.0 bitcast_add_fusion.4
  787.0 5.4 fusion.89
  795.3 9.0 bitcast_add_fusion.4
  813.9 5.3 fusion.89
  822.2 9.0 bitcast_add_fusion.4
  840.7 5.3 fusion.89
  848.9 9.0 bitcast_add_fusion.4
  867.4 5.3 fusion.89
  875.6 8.9 bitcast_add_fusion.4
  884.6 5.3 copy.35
  899.9 40.2 %psum.7 = f32[8192]{0:T(1024)} all-reduce(f32[8192]{0:T(1024)S(1)} %get-tuple-element.743), channel_id=1, replica_groups=mesh['dp'=8,'tensor'=4] {'dp','tensor'}, use_global_device_ids=true, to_apply=%region_13.14 | all-reduce | flops 8192 | bytes 65536 | tf_op jit(solution)/shard_map/psum | solution.py:130
  (249 shorter events, 409.1 us)
Async XLA Ops:
  7.2 6.4 copy-start
  7.2 158.2 %all-gather.6.cloned.1.call-start = ((), (), s32[]{:S(2)}) async-start(), calls=%async_computation.3 | async-start | bytes 10485760 | tf_op jit(solution)/shard_map/all_gather | solution.py:62
  9.3 9.5 %copy-start.2 = (f32[128]{0:T(128)}, f32[128]{0:T(128)S(1)}, u32[]{:S(2)}) copy-start(f32[128]{0:T(128)S(1)} %add_rsqrt_fusion) | copy-start | bytes 1540
  12.8 6.0 copy-start.5
  12.9 7.4 copy-start.4
  12.9 183.3 %all-gather.4.cloned.1.call-start = ((), (), s32[]{:S(2)}) async-start(), calls=%async_computation.2 | async-start | bytes 2949120 | tf_op jit(solution)/shard_map/all_gather | solution.py:73
  14.4 879.8 %reduce-scatter.5.cloned.1.call-start = ((), (), s32[]{:S(2)}) async-start(), calls=%async_computation.5 | async-start | bytes 2949120 | tf_op jit(solution)/shard_map/reduce_scatter | solution.py:124
  670.9 225.2 %reduce-scatter.3.cloned.1.call-start = ((), (), s32[]{:S(2)}) async-start(), calls=%async_computation.4 | async-start | bytes 10485760 | tf_op jit(solution)/shard_map/reduce_scatter | solution.py:121
  889.8 6.3 copy-start.1
  889.8 6.3 copy-start.3
Sparse Core Ops, SparseCore 0:
  13.0 152.3 all-gather.5
  167.8 28.3 all-gather.3
  671.1 43.6 reduce-scatter.4
  717.0 144.4 reduce-scatter.2
where the time goes:
time: 955 us; the launch traced here: 951 us
  matrix products  535 us (56%)
  local copies, waits for them, and re-layouts  159 us (17%)
  waiting for transfers between devices  158 us (17%)
  blocking collectives  49.7 us (5%)
  other arithmetic  33.7 us (4%)
  between operations  15.2 us (2%)
    dot_general x24, matrix products, place_tiles(): jnp.einsum('nsi,sr->nri', lower_half, chooser, preferred_element_type=jnp...  232 us
    all_gather x1, waiting for transfers between devices, body(): gathered = lax.all_gather(normed, 'tensor', axis=0, tiled=True)  136 us
    dot_general x24, matrix products, place_tiles(): jnp.einsum('nsi,sr->nri', upper_half, chooser, preferred_element_type=jnp...  115 us
    dot_general x56, matrix products, pick_tiles(): jnp.einsum('nri,sr->nsi', blocks, chooser, preferred_element_type=jnp.flo...  99.9 us
    convert_element_type x24, local copies, waits for them, and re-layouts, place_tiles(): upper_half = values.astype(jnp.bfloat16)  53.1 us
    psum x1, blocking collectives, body(): gain_grad = lax.psum(gain_part, ('dp', 'tensor'))  40.2 us
    convert_element_type x24, local copies, waits for them, and re-layouts, place_tiles(): lower_half = (values - upper_half.astype(jnp.float32)).astype(jnp.bfloat16)  39.5 us
    dot_general x16, matrix products, tile_group(): jnp.einsum('nsi,nsj->sij', picked_x, picked_g, preferred_element_type=jnp...  38.1 us
  transfers between devices with their start and end apart: 4, of which 2 were waited for; matrix products, arithmetic and copies ran while one was open for 25% of the time, Pallas kernels for 0%

commit v1 on v0

--- a/solution.py
+++ b/solution.py
@@ -1,3 +1,4 @@
+import functools
 import math
 import jax
 import jax.numpy as jnp
@@ -5,6 +6,32 @@
 from jax.sharding import PartitionSpec as P
 
 EPSILON = 1e-05
+
+
+def treat_modes(here_x, a_name, d0):
+    v_next, extra, vec_out = (lax.axis_size(a_name), lax.axis_index(a_name), here_x.shape[d0])
+    all_blocks = list(map(lambda b: (b, (b + 1) % v_next), range(v_next)))
+    xs_all = list(map(lambda b: (b, (b - 1) % v_next), range(v_next)))
+    oldest = jnp.zeros(
+        (*here_x.shape[:d0], v_next * vec_out, *here_x.shape[d0 + 1 :]), here_x.dtype
+    )
+    oldest = lax.dynamic_update_slice_in_dim(oldest, here_x, extra * vec_out, axis=d0)
+    later = u1 = here_x
+    outcome_arr = v_next // 2
+    for dd in range(1, outcome_arr + 1):
+        later = lax.ppermute(later, axis_name=a_name, perm=all_blocks)
+        oldest = lax.dynamic_update_slice_in_dim(
+            oldest, later, (extra - dd) % v_next * vec_out, axis=d0
+        )
+        if dd < v_next - outcome_arr:
+            u1 = lax.ppermute(u1, axis_name=a_name, perm=xs_all)
+            oldest = lax.dynamic_update_slice_in_dim(
+                oldest, u1, (extra + dd) % v_next * vec_out, axis=d0
+            )
+    return oldest
+
+
+find_the_sample = functools.partial(treat_modes, a_name="dp", d0=0)
 
 
 def normalize(source, norm_gain):
@@ -70,7 +97,7 @@
 
     start_out = jnp.zeros((seq_rows, col_tiles, tile_size), jnp.float32)
     all_vals, all_names = (
-        lax.all_gather(masked, "dp", axis=0, tiled=True),
+        find_the_sample(masked),
         lax.all_gather(own_names, "dp", axis=0, tiled=True),
     )
     outputs = over_groups(forward_group, start_out, all_vals, all_names, 0, slot_count)

time: 955 us -> 849 us (0.89)
  matrix products: 535 us -> 403 us
  local copies, waits for them, and re-layouts: 159 us -> 204 us
  waiting for transfers between devices: 158 us -> 128 us
    dot_general x24, matrix products: 232 us -> 147 us  [place_tiles(): jnp.einsum('nsi,sr->nri', lower_half, chooser, preferred_element_type=jnp...]
    dot_general x24, matrix products: 115 us -> 64.1 us  [place_tiles(): jnp.einsum('nsi,sr->nri', upper_half, chooser, preferred_element_type=jnp...]
    all_gather x1, waiting for transfers between devices: 136 us -> 104 us  [body(): gathered = lax.all_gather(normed, 'tensor', axis=0, tiled=True)]
    while x0 -> x65, local copies, waits for them, and re-layouts: none -> 30.5 us
    all_gather x1 -> x0, waiting for transfers between devices: 21.4 us -> none  [body(): lax.all_gather(masked, 'dp', axis=0, tiled=True)]
    ppermute x0 -> x7, waiting for transfers between devices: none -> 17.1 us  [the longest x4 15.7 us: treat_modes(): later = lax.ppermute(later, axis_name=a_name, perm=all_blocks)]
    dot_general x56, matrix products: 99.9 us -> 116 us  [pick_tiles(): jnp.einsum('nri,sr->nsi', blocks, chooser, preferred_element_type=jnp.flo...]
    dot_general x16, matrix products: 34.7 us -> 21.2 us  [backward_group(): jnp.einsum('nsj,sij->nsi', picked_g, block_vals, preferred_element_type=j...]
  transfers between devices with their start and end apart: 4 -> 10, of which waited for: 2 -> 6; matrix products, arithmetic and copies ran while one was open for 25% -> 20% of each run, Pallas kernels for 0% -> 0%
where the time goes in v1:
time: 849 us; the launch traced here: 844 us
  matrix products  403 us (47%)
  local copies, waits for them, and re-layouts  204 us (24%)
  waiting for transfers between devices  128 us (15%)
  blocking collectives  51.2 us (6%)
  other arithmetic  31.7 us (4%)
  between operations  15.3 us (2%)
  starting transfers between devices  9.34 us (1%)
    dot_general x24, matrix products, place_tiles(): jnp.einsum('nsi,sr->nri', lower_half, chooser, preferred_element_type=jnp...  147 us
    dot_general x56, matrix products, pick_tiles(): jnp.einsum('nri,sr->nsi', blocks, chooser, preferred_element_type=jnp.flo...  116 us
    all_gather x1, waiting for transfers between devices, body(): gathered = lax.all_gather(normed, 'tensor', axis=0, tiled=True)  104 us
    dot_general x24, matrix products, place_tiles(): jnp.einsum('nsi,sr->nri', upper_half, chooser, preferred_element_type=jnp...  64.1 us
    convert_element_type x24, local copies, waits for them, and re-layouts, place_tiles(): upper_half = values.astype(jnp.bfloat16)  51 us
    dot_general x16, matrix products, tile_group(): jnp.einsum('nsi,nsj->sij', picked_x, picked_g, preferred_element_type=jnp...  41.9 us
    psum x1, blocking collectives, body(): gain_grad = lax.psum(gain_part, ('dp', 'tensor'))  41.7 us
    convert_element_type x24, local copies, waits for them, and re-layouts, place_tiles(): lower_half = (values - upper_half.astype(jnp.float32)).astype(jnp.bfloat16)  39.5 us
  transfers between devices with their start and end apart: 10, of which 6 were waited for; matrix products, arithmetic and copies ran while one was open for 20% of the time, Pallas kernels for 0%

profile of v1, /device:TPU:0, one launch (start us, length us, event | category | flops | bytes accessed | tf_op | source)
XLA Modules:
  0.0 844.4 jit_solution(4442702809303222131)
XLA Ops:
  18.7 5.6 collective-permute-done
  28.8 4.4 copy.22
  33.3 9.5 %all-reduce = s32[80]{0:T(128)S(1)} all-reduce(s32[80]{0:T(128)S(1)} %bitcast_dynamic-update-slice_fusion.1), channel_id=2, replica_groups=mesh['dp'=8,'tensor'=4] {'dp'}, use_global_device_ids=true, to_apply=%add | all-reduce | flops 80 | bytes 640 | tf_op jit(solution)/shard_map/all_gather | solution.py:101
  53.3 5.9 collective-permute-done.6
  62.2 103.7 %all-gather.3.cloned.1.call-done = bf16[512,8192]{1,0:T(8,128)(2,1)} async-done(((bf16[128,8192]{1,0:T(8,128)(2,1)}), bf16[512,8192]{1,0:T(8,128)(2,1)}) %all-gather.3.cloned.1.call-update) | async-done | bytes 8388624 | tf_op jit(solution)/shard_map/all_gather | solution.py:89
  165.9 9.3 %copy.32 = bf16[64,8,64,128]{3,2,1,0:T(8,128)(2,1)} copy(bf16[64,8,64,128]{3,1,2,0:T(8,128)(2,1)} %bitcast.130) | data formatting | bytes 16777216
  178.3 4.2 broadcast_in_dim.59
  182.6 413.1 %while.101 = (s32[]{:T(128)}, bf16[512,8192]{1,0:T(8,128)(2,1)}, f32[80,128,128]{2,1,0:T(8,128)}, bf16[512,20,128]{0,2,1:T(8,128)(2,1)}, s32[80]{0:T(128)S(1)}, ...) while((s32[]{:T(128)}, bf16[512,8192]{1,0:T(8,128)(2,1)}, ...), condition=%wide.region_8.9_spmd, body=%wide.region_3.8_spmd.sunk | while | flops 329681408 | bytes 87491696 | solution.py:147
  185.1 5.1 constant_dynamic-slice_fusion.5
  190.2 63.1 %while.104 = (s32[]{:T(128)}, f32[80,128,128]{2,1,0:T(8,128)}, s32[80]{0:T(128)S(1)}, bf16[256,64,128]{2,1,0:T(8,128)(2,1)}, bf16[256,20,128]{2,1,0:T(8,128)(2,1...) while((s32[]{:T(128)}, f32[80,128,128]{2,1,0:T(8,128)}, s32[80]{0:T(128)S(1)}, ...), condition=%wide.region_7.7_spmd, body=%wide.region_6.6_spmd.sunk | while | flops 139101120 | bytes 11141467 | solution.py:75
  253.3 121.3 %while.103 = (s32[]{:T(128)}, f32[256,64,128]{2,1,0:T(8,128)}, s32[80]{0:T(128)S(1)}, bf16[80,128,128]{2,1,0:T(8,128)(2,1)}, bf16[256,20,128]{2,1,0:T(8,128)(2,1...) while((s32[]{:T(128)}, f32[256,64,128]{2,1,0:T(8,128)}, s32[80]{0:T(128)S(1)}, ...), condition=%wide.region_5.5_spmd.clone, body=%wide.region_4.4_spmd.clone.sunk | while | flops 188483136 | bytes 41746836 | solution.py:75
  260.5 5.0 bitcast_add_fusion.5
  272.8 8.3 bitcast_add_fusion.5
  288.3 8.3 bitcast_add_fusion.5
  303.9 8.3 bitcast_add_fusion.5
  319.5 8.3 bitcast_add_fusion.5
  335.1 8.3 bitcast_add_fusion.5
  350.7 8.3 bitcast_add_fusion.5
  366.2 8.3 bitcast_add_fusion.5
  374.6 4.5 convert_element_type.269
  379.1 10.0 %bitcast_dynamic-update-slice_fusion.3 = bf16[512,8192]{1,0:T(8,128)(2,1)} fusion(bf16[512,8192]{1,0:T(8,128)(2,1)} %get-tuple-element.1067, s32[]{:T(128)S(6)} %select_n.217, bf16[32,8,64,128]{3,2,1,0:T(8,128)(2,1)S(1)} %bitcast.125), kind=kLoop, calls=%fused_computation.34.clone.1 | loop fusion | bytes 8388612 | tf_op jit(solution)/shard_map/while/body/eval_jaxpr/dynamic_update_slice | solution.py:142
  391.6 5.1 constant_dynamic-slice_fusion.5
  396.7 63.1 %while.104 = (s32[]{:T(128)}, f32[80,128,128]{2,1,0:T(8,128)}, s32[80]{0:T(128)S(1)}, bf16[256,64,128]{2,1,0:T(8,128)(2,1)}, bf16[256,20,128]{2,1,0:T(8,128)(2,1...) while((s32[]{:T(128)}, f32[80,128,128]{2,1,0:T(8,128)}, s32[80]{0:T(128)S(1)}, ...), condition=%wide.region_7.7_spmd, body=%wide.region_6.6_spmd.sunk | while | flops 139101120 | bytes 11141467 | solution.py:75
  459.8 121.3 %while.103 = (s32[]{:T(128)}, f32[256,64,128]{2,1,0:T(8,128)}, s32[80]{0:T(128)S(1)}, bf16[80,128,128]{2,1,0:T(8,128)(2,1)}, bf16[256,20,128]{2,1,0:T(8,128)(2,1...) while((s32[]{:T(128)}, f32[256,64,128]{2,1,0:T(8,128)}, s32[80]{0:T(128)S(1)}, ...), condition=%wide.region_5.5_spmd.clone, body=%wide.region_4.4_spmd.clone.sunk | while | flops 188483136 | bytes 41746836 | solution.py:75
  467.1 5.0 bitcast_add_fusion.5
  479.3 8.3 bitcast_add_fusion.5
  494.9 8.3 bitcast_add_fusion.5
  510.4 8.3 bitcast_add_fusion.5
  526.0 8.3 bitcast_add_fusion.5
  541.6 8.3 bitcast_add_fusion.5
  557.2 8.3 bitcast_add_fusion.5
  572.8 8.3 bitcast_add_fusion.5
  581.1 4.5 convert_element_type.269
  585.6 10.1 %bitcast_dynamic-update-slice_fusion.3 = bf16[512,8192]{1,0:T(8,128)(2,1)} fusion(bf16[512,8192]{1,0:T(8,128)(2,1)} %get-tuple-element.1067, s32[]{:T(128)S(6)} %select_n.217, bf16[32,8,64,128]{3,2,1,0:T(8,128)(2,1)S(1)} %bitcast.125), kind=kLoop, calls=%fused_computation.34.clone.1 | loop fusion | bytes 8388612 | tf_op jit(solution)/shard_map/while/body/eval_jaxpr/dynamic_update_slice | solution.py:142
  595.7 4.5 convert_element_type.186
  600.9 170.0 %while.102 = (s32[]{:T(128)}, f32[512,20,128]{2,1,0:T(8,128)}, s32[80]{0:T(128)S(1)}, bf16[80,128,128]{1,2,0:T(8,128)(2,1)}, bf16[512,64,128]{2,1,0:T(8,128)(2,1...) while((s32[]{:T(128)}, f32[512,20,128]{2,1,0:T(8,128)}, s32[80]{0:T(128)S(1)}, ...), condition=%wide.region_2.3_spmd.clone, body=%wide.region_1.2_spmd.clone.sunk | while | flops 310641792 | bytes 87884280 | solution.py:75
  601.0 4.8 fusion.94
  622.3 4.7 fusion.94
  643.7 4.6 fusion.94
  664.8 4.7 fusion.94
  686.0 4.6 fusion.94
  707.2 4.7 fusion.94
  728.7 4.6 fusion.94
  749.8 4.6 fusion.94
  770.9 5.2 copy.21
  776.1 4.5 copy.25
  782.6 6.5 reduce-scatter.3.cloned.1.call-done
  792.2 41.7 %psum.7 = f32[8192]{0:T(1024)} all-reduce(f32[8192]{0:T(1024)S(1)} %get-tuple-element.727), channel_id=1, replica_groups=mesh['dp'=8,'tensor'=4] {'dp','tensor'}, use_global_device_ids=true, to_apply=%region_13.14 | all-reduce | flops 8192 | bytes 65536 | tf_op jit(solution)/shard_map/psum | solution.py:157
  (362 shorter events, 419.2 us)
Async XLA Ops:
  7.2 7.0 copy-start.4
  7.2 158.8 %all-gather.3.cloned.1.call-start = ((), (), s32[]{:S(2)}) async-start(), calls=%async_computation.2 | async-start | bytes 10485760 | tf_op jit(solution)/shard_map/all_gather | solution.py:89
  13.4 11.4 %copy-start.9 = (u32[32]{0:T(128)S(1)}, u32[32]{0:T(128)}, u32[]{:S(2)}) copy-start(u32[32]{0:T(128)} %constant.336) | copy-start | bytes 388
  13.4 15.3 %copy-start.8 = (s32[1,10]{1,0:T(1,128)S(1)}, s32[1,10]{1,0:T(1,128)}, u32[]{:S(2)}) copy-start(s32[1,10]{1,0:T(1,128)} %param.17) | copy-start | bytes 124
  13.4 767.2 %reduce-scatter.5.cloned.1.call-start = ((), (), s32[]{:S(2)}) async-start(), calls=%async_computation.4 | async-start | bytes 2949120 | tf_op jit(solution)/shard_map/reduce_scatter | solution.py:151
  15.3 9.1 %collective-permute-start = (bf16[10,128,128]{1,2,0:T(8,128)(2,1)S(1)}, bf16[10,128,128]{1,2,0:T(8,128)(2,1)}, u32[]{:S(2)}, u32[]{:S(2)}) collective-permute-start(bf16[10,128,128]{1,2,0:T(8,128)(2,1)S(1)} %get-tuple-element.778), channel_id=1, source_target_pairs={{0,4},{4,8},{8,12},{12,16},{16,20},{20,24},{24,28},{28,0},{1,5},{5... | collective-permute-start | bytes 983048 | tf_op jit(solution)/shard_map/ppermute | solution.py:22
  15.8 10.3 %collective-permute-start.1 = (bf16[10,128,128]{1,2,0:T(8,128)(2,1)S(1)}, bf16[10,128,128]{1,2,0:T(8,128)(2,1)}, u32[]{:S(2)}, u32[]{:S(2)}) collective-permute-start(bf16[10,128,128]{1,2,0:T(8,128)(2,1)S(1)} %get-tuple-element.778), channel_id=1, source_target_pairs={{0,28},{4,0},{8,4},{12,8},{16,12},{20,16},{24,20},{28,24},{1,29},{... | collective-permute-start | bytes 983048 | tf_op jit(solution)/shard_map/ppermute | solution.py:27
  24.4 18.5 %collective-permute-start.2 = (bf16[10,128,128]{1,2,0:T(8,128)(2,1)}, bf16[10,128,128]{1,2,0:T(8,128)(2,1)S(1)}, u32[]{:S(2)}, u32[]{:S(2)}) collective-permute-start(bf16[10,128,128]{1,2,0:T(8,128)(2,1)} %collective-permute-done), channel_id=1, source_target_pairs={{0,4},{4,8},{8,12},{12,16},{16,20},{20,24},{24,28},{28,0},{1,5},{5... | collective-permute-start | bytes 983048 | tf_op jit(solution)/shard_map/ppermute | solution.py:22
  26.1 18.8 %collective-permute-start.3 = (bf16[10,128,128]{1,2,0:T(8,128)(2,1)}, bf16[10,128,128]{1,2,0:T(8,128)(2,1)S(1)}, u32[]{:S(2)}, u32[]{:S(2)}) collective-permute-start(bf16[10,128,128]{1,2,0:T(8,128)(2,1)} %collective-permute-done.1), channel_id=1, source_target_pairs={{0,28},{4,0},{8,4},{12,8},{16,12},{20,16},{24,20},{28,24},{1,29},{... | collective-permute-start | bytes 983048 | tf_op jit(solution)/shard_map/ppermute | solution.py:27
  42.8 9.0 %collective-permute-start.4 = (bf16[10,128,128]{1,2,0:T(8,128)(2,1)S(1)}, bf16[10,128,128]{1,2,0:T(8,128)(2,1)S(1)}, u32[]{:S(2)}, u32[]{:S(2)}) collective-permute-start(bf16[10,128,128]{1,2,0:T(8,128)(2,1)S(1)} %collective-permute-done.2), channel_id=1, source_target_pairs={{0,4},{4,8},{8,12},{12,16},{16,20},{20,24},{24,28},{28,0},{1,5},{5... | collective-permute-start | bytes 983048 | tf_op jit(solution)/shard_map/ppermute | solution.py:22
  44.9 8.3 collective-permute-start.5
  51.8 7.4 collective-permute-start.6
  59.2 116.0 %copy-start.3 = (bf16[80,128,128]{1,2,0:T(8,128)(2,1)}, bf16[80,128,128]{1,2,0:T(8,128)(2,1)S(1)}, u32[]{:S(2)}) copy-start(bf16[80,128,128]{1,2,0:T(8,128)(2,1)S(1)} %constant_dynamic-update-slice_fusion) | copy-start | bytes 7864324
  600.2 188.9 %reduce-scatter.3.cloned.1.call-start = ((), (), s32[]{:S(2)}) async-start(), calls=%async_computation.3 | async-start | bytes 10485760 | tf_op jit(solution)/shard_map/reduce_scatter | solution.py:148
  610.6 5.8 slice-start
  613.5 2.8 slice-start.1
  613.5 3.5 copy-start.1
  619.5 2.7 copy-start
  631.7 5.9 slice-start
  634.7 3.0 slice-start.1
  634.7 3.7 copy-start.1
  640.9 2.7 copy-start
  653.0 5.8 slice-start
  656.0 2.8 slice-start.1
  656.0 3.5 copy-start.1
  662.0 2.7 copy-start
  674.2 5.8 slice-start
  677.2 2.8 slice-start.1
  677.2 3.6 copy-start.1
  683.2 2.7 copy-start
  695.4 5.8 slice-start
  698.4 2.8 slice-start.1
  698.4 3.5 copy-start.1
  704.4 2.7 copy-start
  716.6 5.8 slice-start
  719.5 3.1 slice-start.1
  719.5 3.9 copy-start.1
  725.9 2.7 copy-start
  738.0 5.8 slice-start
  741.0 2.8 slice-start.1
  741.0 3.5 copy-start.1
  747.0 2.7 copy-start
  759.1 5.8 slice-start
  762.1 2.8 slice-start.1
  762.1 3.6 copy-start.1
  776.1 13.0 %copy-start.2 = (bf16[128,8192]{1,0:T(8,128)(2,1)S(1)}, bf16[128,8192]{1,0:T(8,128)(2,1)}, u32[]{:S(2)}) copy-start(bf16[128,8192]{1,0:T(8,128)(2,1)} %param.14) | copy-start | bytes 6291460
  776.1 13.0 %copy-start.5 = (f32[8192]{0:T(1024)S(1)}, f32[8192]{0:T(1024)}, u32[]{:S(2)}) copy-start(f32[8192]{0:T(1024)} %param.15) | copy-start | bytes 98308
  776.1 13.0 %copy-start.7 = (f32[128]{0:T(128)S(1)}, f32[128]{0:T(128)}, u32[]{:S(2)}) copy-start(f32[128]{0:T(128)} %copy-done.6) | copy-start | bytes 1540
  (2 other events, 3.3 us)
Sparse Core Ops, SparseCore 0:
  13.6 152.3 all-gather.2
  600.3 41.8 reduce-scatter.4
  644.6 144.4 reduce-scatter.2
